TPU v7x, 256 devices: a whole 4x4x8 slice. The times are simulated.
256 devices in a mesh: dp: 32 (over z, y_hi, core), tensor: 8 (over y_lo, x).
Axes of the slice: x: 4, y: 4 (y_hi: 2, y_lo: 2; y = y_hi * 2 + y_lo), z: 8, core: 2. Of those that a mesh axis runs over, the one named last changes fastest.
Arguments:
- glu_input: bfloat16 [4096, 2, 3, 1024], P('dp', None, None, 'tensor'), may hold values from -6 to 6
- conv_kernel: bfloat16 [32, 3, 1024], P(None, None, 'tensor'), may hold values from -1 to 1
- norm_gain: float32 [3, 1024], P(None, 'tensor'), may hold values from 0.5 to 2
- norm_shift: float32 [3, 1024], P(None, 'tensor'), may hold values from -3 to 3
- out_weight: bfloat16 [3, 1024, 3, 1024], P(None, 'tensor'), may hold values from -0.109375 to 0.109375
- out_cotangent: bfloat16 [4096, 3, 1024], P('dp'), may hold values from -6 to 6
- root_stack: bfloat16 [16, 2, 1024, 1024], P('tensor', None, 'dp'), as said below
- home: int32 [9], replicated, may hold values from 0 to 15, as said below
Outputs:
- glu_grad: bfloat16 [4096, 2, 3, 1024], P('dp', None, None, 'tensor')
- kernel_grad: float32 [32, 3, 1024], P(None, None, 'tensor')
- update: bfloat16 [3, 1024, 3, 1024], P(None, 'tensor')
Inputs may be any that keep to these rules, and one draw needn't show every extreme that they name: Distinct entries; tensor index home // 2 owns block b. An owner holds at most 2 blocks, and in every draw one owner holds exactly 2. `root_stack`: each of the two matrices in a slot is symmetric.
All inputs are finite; a program needn't handle non-finite values.
Results may differ from a plain program's by a relative error of at most 0.0057.
Values may be sent and summed in bfloat16 or wider, within the bound.
A program may use at most 128 MiB of HBM per device.

v0:
```python
import functools

import jax
import jax.numpy as jnp
from jax import lax
from jax.experimental import pallas as pl
from jax.experimental.pallas import tpu as pltpu
from jax.sharding import PartitionSpec as P

LEN = 2048
MESH = pl.DeviceIdType.MESH
BF = jnp.bfloat16
F32 = jnp.float32

Z = 8
QUADS = 4
TENSOR = 8
TAPS = 32
HALF = TAPS // 2
ROWS = 128
BLOCK = 1024
NB = 3
NBLK = 9
QUART = BLOCK // 4
SHARE = LEN / (ROWS * Z * QUADS)

ORDER = (4, 3, 5, 2, 6, 1, 7, 0)
SPOT = {off: k for k, off in enumerate(ORDER)}
HOPS = ((4, 3), (3, 4))


def dot(a, b, dims):
    return lax.dot_general(a, b, (dims, ((), ())), preferred_element_type=F32)


def keep(dst, at, src, m):
    dst[at] = src[m]


def kernel(
    home, glu_hbm, weight_hbm, cot_hbm, roots_hbm, taps, gain, shift,
    upd, kgrad, ggrad,
    raw, glu, cot, roots, tapf, cand, rpick, lpick, rrows, rfull, lfull, lturn,
    halo, cg_halo, gext, normed_s, cg_b, cgext, weight,
    acts, ycols, gacc, relay, zsend, zrecv, erecv, gfull, wall,
    kpart, kin1, ksend2, kin2, ksum, kz, khalf,
    raw_sem, w_sem, cot_sem, roots_sem, halo_s, halo_r, s1_s, s1_r, r2_s, r2_r, l2_s, l2_r,
    r3_s, r3_r, l3_s, l3_r, yc_s, yc_r, ys_s, ys_r, yx_s, yx_r, at_s, at_r, yc_own, z_s, z_r, ez_s, ez_r,
    c_s, c_r, wt_s, wt_r, uz_s, uz_r, uy_s, uy_r, us_s, us_r, ch_s, ch_r, k_s, k_r,
):
    d = lax.axis_index("dp")
    t = lax.axis_index("tensor")
    z = lax.div(d, 4)
    a = lax.rem(d, 4)
    yh = lax.div(a, 2)
    c = lax.rem(a, 2)
    sib = d + 1 - 2 * c
    par = d + 2 - 4 * yh

    def at_z(zz):
        return lax.rem(zz + 2 * Z, Z) * 4 + a

    quad = 2 * c + yh
    home_z = z == t

    def diagonal(m):
        tt = lax.rem(t + m, TENSOR)
        return (tt * 4 + a, tt)

    sends = []

    def send(src, dst, ss, rs, dev, when=None):
        copy = pltpu.make_async_remote_copy(
            src_ref=src, dst_ref=dst, send_sem=ss, recv_sem=rs,
            device_id=dev, device_id_type=MESH,
        )
        if when is None:
            copy.start()
        else:
            pl.when(when)(copy.start)
        sends.append((copy, when))

    def got(dst, rs):
        pltpu.make_async_remote_copy(
            src_ref=dst, dst_ref=dst, send_sem=s1_s.at[0], recv_sem=rs,
            device_id=(sib, t), device_id_type=MESH,
        ).wait_recv()

    barrier = pltpu.get_barrier_semaphore()

    def hello(dev):
        pl.semaphore_signal(barrier, inc=1, device_id=dev, device_id_type=MESH)

    hello((lax.rem(d + 31, 32), t))
    hello((lax.rem(d + 1, 32), t))
    for m in range(1, 4):
        hello((z * 4 + lax.rem(a + m, 4), t))
    for m in range(1, Z):
        hello((at_z(z + m), t))
    for m in range(1, TENSOR):
        hello((d, lax.rem(t + m, TENSOR)))

    r_quad = lax.div(z, 2)
    r_to = lax.rem(r_quad, 2) * 2 + lax.div(r_quad, 2)
    r_slot = lax.rem(z, 2) * 4 + a

    for n in range(Z):
        pl.when(8 * quad + n != d)(functools.partial(hello, (8 * quad + n, t)))
    for m in range(1, TENSOR):
        pl.when(home_z)(functools.partial(hello, diagonal(m)))

    raw_copy = pltpu.make_async_copy(glu_hbm, raw, raw_sem)
    raw_copy.start()
    roots_copy = pltpu.make_async_copy(roots_hbm, roots, roots_sem)
    roots_copy.start()
    cot_copy = pltpu.make_async_copy(cot_hbm, cot, cot_sem)
    cot_copy.start()
    w_copy = pltpu.make_async_copy(weight_hbm, weight, w_sem)
    w_copy.start()

    left_ok = (d != 0) & (lax.rem(d * ROWS + LEN // 2, LEN) != 0)
    right_ok = (d != 31) & (lax.rem((d + 1) * ROWS + LEN // 2, LEN) != 0)
    raw_copy.wait()

    def halves(i):
        both = raw[:, i].astype(F32)
        return both[:, 0, :], both[:, 1, :]

    for i in range(NB):
        lin, gate = halves(i)
        glu[i] = (lin * jax.nn.sigmoid(gate)).astype(BF)
        gext[i, HALF:HALF + ROWS, :] = glu[i].astype(F32)
        tapf[i] = taps[i].astype(F32)

    more = jnp.where(home_z, TENSOR - 1, 0) - jnp.where(r_to == a, 1, 0)
    pl.semaphore_wait(barrier, 2 + 3 + Z - 1 + TENSOR - 1 + Z + more)

    dn, up = (lax.rem(d + 31, 32), t), (lax.rem(d + 1, 32), t)
    send(glu.at[:, 0:HALF], halo.at[1], halo_s.at[0], halo_r.at[1], dn, left_ok)
    send(glu.at[:, ROWS - HALF:ROWS], halo.at[0], halo_s.at[1], halo_r.at[0], up, right_ok)
    roots_copy.wait()
    def quad_of(aa):
        return 2 * lax.rem(aa, 2) + lax.div(aa, 2)

    def quad_cols(aa):
        return pl.ds(pl.multiple_of(quad_of(aa) * QUART, QUART), QUART)

    def frames_of(aa):
        return pl.ds(pl.multiple_of(aa * ROWS, ROWS), ROWS)

    my_frames = frames_of(a)
    y_own = pltpu.make_async_copy(cot_hbm.at[:, :, quad_cols(a)], ycols.at[:, my_frames], yc_own)
    y_own.start()
    a_par, a_sib, a_far = a + 2 - 4 * yh, a + 1 - 2 * c, 3 - a
    my_x = lax.rem(t, 4)

    def piece_of(aa, xx):
        rows = pl.ds(pl.multiple_of(aa * ROWS + xx * 32, 32), 32)
        return ycols.at[:, rows]

    x_rows = pl.ds(pl.multiple_of(my_x * 32, 32), 32)
    for n, aa in enumerate((a_par, a_far)):
        src = cot_hbm.at[:, x_rows, quad_cols(aa)]
        send(src, piece_of(a, my_x), yc_s.at[n], yc_r.at[n], (z * 4 + aa, t))
    src = cot_hbm.at[:, :, quad_cols(a_sib)]
    send(src, ycols.at[:, my_frames], ys_s.at[0], ys_r.at[0], (sib, t))

    for m in range(1, TENSOR):
        tt = lax.rem(t + m, TENSOR)
        share_cols = pl.ds(pl.multiple_of(tt * ROWS, ROWS), ROWS)
        send(roots.at[:, :, :, share_cols], cand.at[t], s1_s.at[m], s1_r.at[m], (d, tt))
    cand[t] = roots[:, :, :, pl.ds(pl.multiple_of(t * ROWS, ROWS), ROWS)]

    def rim(side, ok, sem, src, dst, rows):
        @pl.when(ok)
        def _():
            got(src.at[side], sem.at[side])
            for i in range(NB):
                dst[i, rows, :] = src[side, i].astype(F32)

        @pl.when(jnp.logical_not(ok))
        def _():
            for i in range(NB):
                dst[i, rows, :] = jnp.zeros((HALF, ROWS), F32)

    low, high = pl.ds(0, HALF), pl.ds(HALF + ROWS, HALF)
    rim(0, left_ok, halo_r, halo, gext, low)
    rim(1, right_ok, halo_r, halo, gext, high)

    for n, aa in enumerate((a_par, a_far)):
        src = piece_of(aa, my_x)
        got(src, yc_r.at[n])
        for m in range(1, 4):
            dev = (d, t - my_x + lax.rem(my_x + m, 4))
            send(src, src, yx_s.at[n, m], yx_r.at[n, m], dev)

    def conv(i, carry):
        total = jnp.zeros((ROWS, ROWS), F32)
        for j in range(TAPS):
            total = total + tapf[i, j:j + 1, :] * gext[i, j:j + ROWS, :]
        normed = total * gain[pl.ds(i, 1), :] + shift[pl.ds(i, 1), :]
        normed_s[i] = normed
        acts[i, :, my_frames] = (normed * jax.nn.sigmoid(normed)).T.astype(BF)
        return carry

    lax.fori_loop(0, NB, conv, 0)


    def acts_of(aa):
        return acts.at[:, :, frames_of(aa)]

    send(acts_of(a), acts_of(a), at_s.at[0], at_r.at[0], (par, t))
    send(acts_of(a), acts_of(a), at_s.at[1], at_r.at[1], (sib, t))

    for m in range(1, TENSOR):
        got(cand.at[lax.rem(t + m, TENSOR)], s1_r.at[TENSOR - m])
    r_rows = pl.ds(pl.multiple_of(r_slot * 32, 32), 32)
    for m in range(NBLK):
        x = m // Z
        zz = t if x else lax.rem(z + m, Z)
        slot = home[8 if x else zz]
        own, which = lax.shift_right_logical(slot, 1), slot & 1
        lpick[m] = cand[own, which, 0]
        rpick[m] = cand[own, which, 1]
        r_dev = zz * 4 + r_to
        l_dev = zz * 4 + a
        send(rpick.at[m], rrows.at[x, r_rows], r2_s.at[m], r2_r.at[x, r_slot], (r_dev, t), r_dev != d)
        pl.when(r_dev == d)(functools.partial(keep, rrows, (x, r_rows), rpick, m))
        send(lpick.at[m], lfull.at[x, z, a], l2_s.at[m], l2_r.at[x, z], (l_dev, t), l_dev != d)
        pl.when(l_dev == d)(functools.partial(keep, lfull, (x, z, a), lpick, m))

    off_relay, off_plain = 2 + 4 * c, 6 - 4 * c
    offs = (4, 3, 5, None, off_plain, 1, 7, 0, off_relay)

    def product(n, chip):
        block = Z if n == 3 else lax.rem(z + offs[n], Z)
        row, col = (2, 2) if n == 3 else (lax.div(block, NB), lax.rem(block, NB))
        span = pl.ds(pl.multiple_of(chip * 256, 256), 256)
        return dot(acts[row, :, span], ycols[col, span, :], ((1,), (0,)))

    y_own.wait()
    got(ycols.at[:, frames_of(a_sib)], ys_r.at[0])
    got(acts_of(a_sib), at_r.at[1])
    for n in range(NBLK):
        gacc[n] = product(n, yh)

    got(acts_of(a_par), at_r.at[0])
    send(acts_of(a_par), acts_of(a_par), at_s.at[2], at_r.at[2], (sib, t))
    for n, aa in enumerate((a_par, a_far)):
        for m in range(1, 4):
            got(piece_of(aa, lax.rem(my_x + 4 - m, 4)), yx_r.at[n, m])
    got(acts_of(a_far), at_r.at[2])

    e_off = lax.rem(z - t + Z, Z)
    e_far = (e_off > 1) & (e_off < 7)
    e_low = (e_off < 4) | ((e_off == 4) & (c == 0))
    e_via = at_z(jnp.where(e_low, t + 1, t - 1))

    def e_merge(sources, odd):
        for n in sources:
            got(erecv.at[n], ez_r.at[n])

        @pl.when(c == odd)
        def _():
            got(erecv.at[4], ez_r.at[4])

        @pl.when(c != odd)
        def _():
            erecv[4] = jnp.zeros((ROWS, QUART), BF)

        total = gacc[3] + erecv[4].astype(F32)
        for n in sources:
            total = total + erecv[n].astype(F32)
        zsend[3] = total.astype(BF)

    my_cols = pl.ds(pl.multiple_of(t * ROWS, ROWS), ROWS)

    def roots_in(x):
        for n in range(Z):
            source = 8 * quad + n
            rows = pl.ds(32 * n, 32)
            pl.when(source != d)(functools.partial(got, rrows.at[x, rows], r2_r.at[x, n]))
            pl.when(z != n)(functools.partial(got, lfull.at[x, n, a], l2_r.at[x, n]))
        rfull[x, :, my_cols] = rrows[x]

    def roots_out(x, when):
        for m in range(1, TENSOR):
            dev = diagonal(m) if x else (d, lax.rem(t + m, TENSOR))
            send(rrows.at[x], rfull.at[x, :, my_cols], r3_s.at[x, m], r3_r.at[x, m], dev, when)
        mine = lfull.at[x, :, a]
        send(mine, mine, l3_s.at[x, 0], l3_r.at[x, 0], (par, t), when)
        send(mine, mine, l3_s.at[x, 1], l3_r.at[x, 1], (sib, t), when)

    def left_on(x, when):
        his = lfull.at[x, :, a_par]
        if when is None:
            got(his, l3_r.at[x, 0])
        else:
            pl.when(when)(functools.partial(got, his, l3_r.at[x, 0]))
        send(his, his, l3_s.at[x, 2], l3_r.at[x, 2], (sib, t), when)

    for n in range(NBLK):
        if n == 3:
            roots_in(0)
            roots_out(0, None)
            pl.when(home_z)(functools.partial(roots_in, 1))
            roots_out(1, home_z)
        total = gacc[n] + product(n, 1 - yh)
        if n == 3:
            gacc[n] = total
            zsend[n] = total.astype(BF)
            send(zsend.at[n], erecv.at[e_off], ez_s.at[0], ez_r.at[e_off], (e_via, t), e_far)
        elif n == 0:
            zsend[n] = total.astype(BF)
            send(zsend.at[n], relay, z_s.at[n], z_r.at[4], (at_z(z + off_relay), t))
        elif n == 7:
            gacc[n] = total
        else:
            if n == 8:
                got(relay, z_r.at[4])
                total = total + relay[...].astype(F32)
            zsend[n] = total.astype(BF)
            send(
                zsend.at[n], zrecv.at[offs[n]], z_s.at[n], z_r.at[offs[n]],
                (at_z(z + offs[n]), t),
            )

    pl.when(e_off == 1)(functools.partial(e_merge, (2, 3), 0))
    pl.when(e_off == 7)(functools.partial(e_merge, (5, 6), 1))
    near = (e_off == 1) | (e_off == 7)
    send(zsend.at[3], erecv.at[e_off], ez_s.at[0], ez_r.at[e_off], (at_z(t), t), near)

    cot_copy.wait()
    w_copy.wait()
    for i in range(NB):
        grad = jnp.zeros((ROWS, ROWS), F32)
        for j in range(NB):
            grad = grad + dot(cot[j], weight[i, j], ((1,), (1,)))
        normed = normed_s[i]
        sg = jax.nn.sigmoid(normed)
        cg = (grad * sg * (1.0 + normed * (1.0 - sg)) * gain[i:i + 1, :]).astype(BF)
        cg_b[i] = cg
        cgext[i, HALF:HALF + ROWS, :] = cg.astype(F32)
    send(cg_b.at[:, 0:HALF], cg_halo.at[1], ch_s.at[0], ch_r.at[1], dn, left_ok)
    send(cg_b.at[:, ROWS - HALF:ROWS], cg_halo.at[0], ch_s.at[1], ch_r.at[0], up, right_ok)

    left_on(0, None)
    left_on(1, home_z)

    def tap_grad(i, carry):
        cg = cgext[i, HALF:HALF + ROWS, :]
        for j in range(TAPS):
            terms = (cg * gext[i, j:j + ROWS, :]).reshape(ROWS // 8, 8, ROWS)
            row = jnp.sum(jnp.sum(terms, axis=0), axis=0, keepdims=True)
            kpart[j // HALF, i, j % HALF:j % HALF + 1, :] = row
        return carry

    lax.fori_loop(0, NB, tap_grad, 0)
    send(kpart.at[1 - c], kin1, k_s.at[0], k_r.at[0], (sib, t))

    def roots_all(x):
        for m in range(1, TENSOR):
            tt = lax.rem(t + m, TENSOR)
            cols = pl.ds(pl.multiple_of(tt * ROWS, ROWS), ROWS)
            got(rfull.at[x, :, cols], r3_r.at[x, TENSOR - m])
        got(lfull.at[x, :, a_sib], l3_r.at[x, 1])
        got(lfull.at[x, :, a_far], l3_r.at[x, 2])
        for zz in range(Z):
            part = lfull[x, zz].reshape(ROWS, ROWS).astype(F32)
            lturn[x, :, ROWS * zz:ROWS * zz + ROWS] = part.T.astype(BF)

    def join(x):
        total = gacc[3 if x else 7]
        for n in range(Z):
            if x == 0 and n not in (0, 4):
                got(zrecv.at[n], z_r.at[n])
                total = total + zrecv[n].astype(F32)
            elif x == 1 and n in (1, 7):
                got(erecv.at[n], ez_r.at[n])
                total = total + erecv[n].astype(F32)
        gfull[x, quad] = total.astype(BF)

    par_quad = 2 * c + 1 - yh

    def quarters_out(x, when):
        mine = gfull.at[x, quad]
        send(mine, mine, c_s.at[x, 0], c_r.at[x, 0], (par, t), when)
        send(mine, mine, c_s.at[x, 1], c_r.at[x, 1], (sib, t), when)

    def quarters_on(x, when):
        his = gfull.at[x, par_quad]
        send(his, his, c_s.at[x, 2], c_r.at[x, 2], (sib, t), when)

    def quarters_in(x):
        got(gfull.at[x, 2 * (1 - c) + yh], c_r.at[x, 1])
        got(gfull.at[x, 2 * (1 - c) + 1 - yh], c_r.at[x, 2])

    join(0)
    quarters_out(0, None)
    pl.when(home_z)(functools.partial(join, 1))
    quarters_out(1, home_z)

    got(kin1, k_r.at[0])
    ksend2[...] = kpart[c] + kin1[...]
    send(ksend2, kin2, k_s.at[1], k_r.at[1], (par, t))

    roots_all(0)
    pl.when(home_z)(functools.partial(roots_all, 1))

    got(gfull.at[0, par_quad], c_r.at[0, 0])
    quarters_on(0, None)
    pl.when(home_z)(functools.partial(got, gfull.at[1, par_quad], c_r.at[1, 0]))
    quarters_on(1, home_z)
    quarters_in(0)

    def right(x):
        part = jnp.zeros((ROWS, QUART), F32)
        for q in range(QUADS):
            part = part + dot(gfull[x, q], rfull[x, :, QUART * q:QUART * q + QUART], ((1,), (1,)))
        wall[x, t] = (part * SHARE).astype(BF)

    right(0)
    for m in range(1, TENSOR):
        dev = (d, lax.rem(t + m, TENSOR))
        send(wall.at[0, t], wall.at[0, t], wt_s.at[0, m], wt_r.at[0, m], dev)

    @pl.when(home_z)
    def _():
        quarters_in(1)
        right(1)

    for m in range(1, TENSOR):
        send(wall.at[1, t], wall.at[1, t], wt_s.at[1, m], wt_r.at[1, m], diagonal(m), home_z)

    got(kin2, k_r.at[1])
    ksum[...] = ksend2[...] + kin2[...]
    for m in range(1, Z):
        send(ksum, kz.at[z], k_s.at[1 + m], k_r.at[1 + m], (at_z(z + m), t))
    kz[z] = ksum[...]

    rim(0, left_ok, ch_r, cg_halo, cgext, low)
    rim(1, right_ok, ch_r, cg_halo, cgext, high)

    for i in range(NB):
        total = jnp.zeros((ROWS, ROWS), F32)
        for j in range(TAPS):
            total = total + tapf[i, j:j + 1, :] * cgext[i, TAPS - j:TAPS - j + ROWS, :]
        lin, gate = halves(i)
        sg = jax.nn.sigmoid(gate)
        total = total * sg
        ggrad[:, i, 0, :] = total.astype(BF)
        ggrad[:, i, 1, :] = (total * lin * (1.0 - sg)).astype(BF)

    def quarter(block, q):
        cols = pl.ds(pl.multiple_of(q * QUART, QUART), QUART)
        return upd.at[lax.div(block, NB), lax.rem(block, NB), :, cols]

    def left_mult(x, block):
        for m in range(1, TENSOR):
            got(wall.at[x, lax.rem(t + m, TENSOR)], wt_r.at[x, TENSOR - m])
        part = dot(lturn[x], wall[x].reshape(BLOCK, QUART), ((1,), (0,)))
        quarter(block, quad)[...] = part.astype(BF)

    second = jnp.int32(Z)
    sib_quads = (2 * (1 - c) + yh, 2 * (1 - c) + 1 - yh)

    def piece(n, q):
        return quarter(second if n == Z else lax.rem(z + n, Z), q)

    def on(n, h, when=None):
        src = piece(n, par_quad if h else quad)
        if h == 0 and n not in (1, 7):
            send(src, src, uy_s.at[n], uy_r.at[n], (par, t), when)
        send(src, src, us_s.at[n, h], us_r.at[n, h], (sib, t), when)

    left_mult(0, z)
    for off in (3, 5, 2, 6, 1, 7):
        src = piece(0, quad)
        send(src, src, uz_s.at[off], uz_r.at[off], (at_z(z + off), t))
    on(0, 0)

    @pl.when(home_z)
    def _():
        left_mult(1, second)

    for off in (3, 5, 2, 6, 1, 7):
        src = piece(Z, quad)
        send(src, src, uz_s.at[Z + off], uz_r.at[Z], (at_z(z + off), t), home_z)

    for m in range(1, Z):
        got(kz.at[lax.rem(z + m, Z)], k_r.at[1 + Z - m])
    total = kz[0]
    for zz in range(1, Z):
        total = total + kz[zz]
    khalf[c] = total * SHARE
    send(khalf.at[c], khalf.at[c], k_s.at[9], k_r.at[9], (sib, t))

    got(piece(0, par_quad), uy_r.at[0])
    for off in (1, 7):
        src = piece(0, par_quad)
        send(src, src, uy_s.at[off], uy_r.at[Z - off], (at_z(z + off), t))
    on(0, 1)

    def pass_on(n, land, when):
        src = piece(n, quad)
        send(src, src, uz_s.at[4 + land], uz_r.at[land], (at_z(z - 1 + 2 * c), t), when)

    for off in (3, 5, 2, 6, 1, 7):
        got(piece(off, quad), uz_r.at[Z - off])
        if off == 3:
            pass_on(3, 4, c == 0)
        if off == 5:
            pass_on(5, 4, c == 1)
        on(off, 0)
    pl.when(jnp.logical_not(home_z))(functools.partial(got, piece(Z, quad), uz_r.at[Z]))
    pass_on(Z, Z, lax.rem(t - z + Z, Z) == 3 + 2 * c)
    on(Z, 0)
    got(piece(4, quad), uz_r.at[4])
    on(4, 0)
    for n in (1, 7, 3, 5, 2, 6, Z, 4):
        got(piece(n, par_quad), uy_r.at[n])
        on(n, 1)

    got(khalf.at[1 - c], k_r.at[9])
    for half in range(2):
        for i in range(NB):
            kgrad[i, HALF * half:HALF * half + HALF, :] = khalf[half, i]

    for n in range(Z + 1):
        for h in range(2):
            got(piece(n, sib_quads[h]), us_r.at[n, h])

    for copy, when in sends:
        if when is None:
            copy.wait_send()
        else:
            pl.when(when)(copy.wait_send)


def hand_over(upd, kgrad, ggrad, upd_out, kgrad_out, ggrad_out, upd_v, kgrad_v, ggrad_v, ins, outs):
    legs = [(kgrad, kgrad_v, kgrad_out), (ggrad, ggrad_v, ggrad_out)]
    for b in range(NBLK):
        at = (b // NB, b % NB)
        legs.append((upd.at[at], upd_v.at[at], upd_out.at[at]))
    arrive = [pltpu.make_async_copy(x, y, ins.at[n]) for n, (x, y, _) in enumerate(legs)]
    leave = [pltpu.make_async_copy(y, w, outs.at[n]) for n, (_, y, w) in enumerate(legs)]
    for copy in arrive:
        copy.start()
    for copy, then in zip(arrive, leave):
        copy.wait()
        then.start()
    for copy in leave:
        copy.wait()


def per_device(
    glu_input, conv_kernel, norm_gain, norm_shift, out_weight, out_cotangent, root_stack, home
):
    vmem = pl.BlockSpec(memory_space=pltpu.VMEM)
    hbm = pl.BlockSpec(memory_space=pltpu.HBM)
    dma = pltpu.SemaphoreType.DMA
    sq = (NB, ROWS, ROWS)
    out = pl.pallas_call(
        kernel,
        out_shape=(
            jax.ShapeDtypeStruct((NB, NB, ROWS, BLOCK), BF),
            jax.ShapeDtypeStruct((NB, TAPS, ROWS), F32),
            jax.ShapeDtypeStruct((ROWS, NB, 2, ROWS), BF),
        ),
        in_specs=[
            pl.BlockSpec(memory_space=pltpu.SMEM), hbm, hbm, hbm, hbm, vmem, vmem, vmem,
        ],
        out_specs=(vmem, vmem, vmem),
        scratch_shapes=[
            pltpu.VMEM((ROWS, NB, 2, ROWS), BF),
            pltpu.VMEM(sq, BF),
            pltpu.VMEM((NB, ROWS, BLOCK), BF),
            pltpu.VMEM((2, 2, 32, BLOCK), BF),
            pltpu.VMEM((NB, TAPS, ROWS), F32),
            pltpu.VMEM((TENSOR, 2, 2, 32, ROWS), BF),
            pltpu.VMEM((NBLK, 32, ROWS), BF),
            pltpu.VMEM((NBLK, 32, ROWS), BF),
            pltpu.VMEM((2, QUART, ROWS), BF),
            pltpu.VMEM((2, QUART, BLOCK), BF),
            pltpu.VMEM((2, Z, QUADS, 32, ROWS), BF),
            pltpu.VMEM((2, ROWS, BLOCK), BF),
            pltpu.VMEM((2, NB, HALF, ROWS), BF),
            pltpu.VMEM((2, NB, HALF, ROWS), BF),
            pltpu.VMEM((NB, ROWS + TAPS, ROWS), F32),
            pltpu.VMEM(sq, F32),
            pltpu.VMEM(sq, BF),
            pltpu.VMEM((NB, ROWS + TAPS, ROWS), F32),
            pltpu.VMEM((NB, NB, ROWS, BLOCK), BF),
            pltpu.VMEM((NB, ROWS, QUADS * ROWS), BF),
            pltpu.VMEM((NB, QUADS * ROWS, QUART), BF),
            pltpu.VMEM((NBLK, ROWS, QUART), F32),
            pltpu.VMEM((ROWS, QUART), BF),
            pltpu.VMEM((NBLK, ROWS, QUART), BF),
            pltpu.VMEM((Z, ROWS, QUART), BF),
            pltpu.VMEM((Z, ROWS, QUART), BF),
            pltpu.VMEM((2, QUADS, ROWS, QUART), BF),
            pltpu.VMEM((2, TENSOR, ROWS, QUART), BF),
            pltpu.VMEM((2, NB, HALF, ROWS), F32),
            pltpu.VMEM((NB, HALF, ROWS), F32),
            pltpu.VMEM((NB, HALF, ROWS), F32),
            pltpu.VMEM((NB, HALF, ROWS), F32),
            pltpu.VMEM((NB, HALF, ROWS), F32),
            pltpu.VMEM((Z, NB, HALF, ROWS), F32),
            pltpu.VMEM((2, NB, HALF, ROWS), F32),
            dma, dma, dma, dma,
            dma((2,)), dma((2,)),
            dma((8,)), dma((8,)),
            dma((9,)), dma((2, 8)),
            dma((9,)), dma((2, 8)),
            dma((2, 8)), dma((2, 8)),
            dma((2, 4)), dma((2, 4)),
            dma((2,)), dma((2,)),
            dma((1,)), dma((1,)),
            dma((2, 4)), dma((2, 4)),
            dma((3,)), dma((3,)),
            dma,
            dma((9,)), dma((8,)),
            dma((1,)), dma((8,)),
            dma((2, 3)), dma((2, 3)),
            dma((2, 8)), dma((2, 8)),
            dma((16,)), dma((9,)),
            dma((9,)), dma((9,)),
            dma((9, 2)), dma((9, 2)),
            dma((2,)), dma((2,)),
            dma((10,)), dma((10,)),
        ],
        compiler_params=pltpu.CompilerParams(
            collective_id=0, has_side_effects=True, vmem_limit_bytes=60 * 2**20
        ),
    )(
        home, glu_input.transpose(0, 2, 1, 3), out_weight.transpose(0, 2, 1, 3), out_cotangent.transpose(1, 0, 2),
        root_stack, conv_kernel.transpose(1, 0, 2), norm_gain, norm_shift,
    )
    update, kernel_grad, glu_grad = pl.pallas_call(
        hand_over,
        out_shape=[jax.ShapeDtypeStruct(x.shape, x.dtype) for x in out],
        in_specs=[hbm] * 3,
        out_specs=[hbm] * 3,
        scratch_shapes=[pltpu.VMEM(x.shape, x.dtype) for x in out]
        + [dma((NBLK + 2,)), dma((NBLK + 2,))],
        compiler_params=pltpu.CompilerParams(vmem_limit_bytes=60 * 2**20),
    )(*out)
    return glu_grad.transpose(0, 2, 1, 3), kernel_grad.transpose(1, 0, 2), update.transpose(0, 2, 1, 3)


def solution(mesh):
    placed = (
        P("dp", None, None, "tensor"),
        P(None, None, "tensor"),
        P(None, "tensor"),
        P(None, "tensor"),
        P(None, "tensor", None, None),
        P("dp", None, None),
        P("tensor", None, "dp", None),
        P(),
    )
    return jax.shard_map(
        per_device,
        mesh=mesh,
        in_specs=placed,
        out_specs=(
            P("dp", None, None, "tensor"),
            P(None, None, "tensor"),
            P(None, "tensor", None, None),
        ),
        check_vma=False,
    )
```

profile of v0, /device:TPU:9, one launch (start us, length us, event | category | flops | bytes accessed | tf_op | source)
XLA Modules:
  0.0 87.3 jit_solution(472147436433300178)
XLA Ops:
  0.6 84.0 %shard_map.103 = (bf16[3,3,128,1024]{3,2,1,0:T(8,128)(2,1)}, f32[3,32,128]{2,1,0:T(8,128)}, bf16[128,3,2,128]{3,2,1,0:T(2,128)(2,1)}) custom-call(s32[9]{0:T(128)} %home.1, bf16[128,3,2,128]{3,2,1,0:T(2,128)(2,1)} %bitcast.9, bf16[3,3,128,1024]{3,2,1,0:T(8,128)(2,1)} %bitcast.7, bf16[3,128,1024]{2,1,0:T(8,128)(2,1)} %bitcast.8, ...), custom_call_target="tpu_custom_call" | custom-call | tf_op jit(solution)/shard_map/pallas_call | solution.py:563
  84.6 2.7 %shard_map.104 = (bf16[3,3,128,1024]{3,2,1,0:T(8,128)(2,1)}, f32[3,32,128]{2,1,0:T(8,128)}, bf16[128,3,2,128]{3,2,1,0:T(2,128)(2,1)}) custom-call(bf16[3,3,128,1024]{3,2,1,0:T(8,128)(2,1)} %get-tuple-element.9.upd, f32[3,32,128]{2,1,0:T(8,128)} %get-tuple-element.10.kgrad, bf16[128,3,2,128]{3,2,1,0:T(2,128)(2,1)} %get-tuple-element.11.ggrad), custom_call_target="tpu_custom_call" | custom-call | tf_op jit(solution)/shard_map/pallas_call | solution.py:639
where the time goes:
time: 87.4 us; the launch traced here: 87.3 us
  Pallas kernels  86.6 us (99%)
    pallas_call x1, Pallas kernels, per_device(): pl.pallas_call(kernel, out_shape=(jax.ShapeDtypeStruct((NB, NB, ROWS, BLO...  84 us
    pallas_call x1, Pallas kernels, per_device(): pl.pallas_call(hand_over, out_shape=[jax.ShapeDtypeStruct(x.shape, x.dtyp...  2.66 us

commit v1 on v0

--- a/solution.py
+++ b/solution.py
@@ -203,14 +203,15 @@
         acts[i, :, my_frames] = (normed * jax.nn.sigmoid(normed)).T.astype(BF)
         return carry
 
-    lax.fori_loop(0, NB, conv, 0)
-
 
     def acts_of(aa):
         return acts.at[:, :, frames_of(aa)]
 
-    send(acts_of(a), acts_of(a), at_s.at[0], at_r.at[0], (par, t))
-    send(acts_of(a), acts_of(a), at_s.at[1], at_r.at[1], (sib, t))
+    for i in range(NB):
+        conv(i, 0)
+        mine = acts.at[i, :, my_frames]
+        send(mine, mine, at_s.at[i], at_r.at[i], (par, t))
+    send(acts_of(a), acts_of(a), at_s.at[3], at_r.at[3], (sib, t))
 
     for m in range(1, TENSOR):
         got(cand.at[lax.rem(t + m, TENSOR)], s1_r.at[TENSOR - m])
@@ -240,16 +241,19 @@
 
     y_own.wait()
     got(ycols.at[:, frames_of(a_sib)], ys_r.at[0])
-    got(acts_of(a_sib), at_r.at[1])
+    got(acts_of(a_sib), at_r.at[3])
     for n in range(NBLK):
         gacc[n] = product(n, yh)
 
-    got(acts_of(a_par), at_r.at[0])
-    send(acts_of(a_par), acts_of(a_par), at_s.at[2], at_r.at[2], (sib, t))
+    for i in range(NB):
+        his = acts.at[i, :, frames_of(a_par)]
+        got(his, at_r.at[i])
+        send(his, his, at_s.at[4 + i], at_r.at[4 + i], (sib, t))
     for n, aa in enumerate((a_par, a_far)):
         for m in range(1, 4):
             got(piece_of(aa, lax.rem(my_x + 4 - m, 4)), yx_r.at[n, m])
-    got(acts_of(a_far), at_r.at[2])
+    for i in range(NB):
+        got(acts.at[i, :, frames_of(a_far)], at_r.at[4 + i])
 
     e_off = lax.rem(z - t + Z, Z)
     e_far = (e_off > 1) & (e_off < 7)
@@ -300,7 +304,7 @@
         send(his, his, l3_s.at[x, 2], l3_r.at[x, 2], (sib, t), when)
 
     for n in range(NBLK):
-        if n == 3:
+        if n == 8:
             roots_in(0)
             roots_out(0, None)
             pl.when(home_z)(functools.partial(roots_in, 1))
@@ -617,7 +621,7 @@
             dma((2,)), dma((2,)),
             dma((1,)), dma((1,)),
             dma((2, 4)), dma((2, 4)),
-            dma((3,)), dma((3,)),
+            dma((7,)), dma((7,)),
             dma,
             dma((9,)), dma((8,)),
             dma((1,)), dma((8,)),

time: 87.4 us -> 87 us (level)
  no operation moved by 1% of the time
where the time goes in v1:
time: 87 us; the launch traced here: 86.7 us
  Pallas kernels  86 us (99%)
    pallas_call x1, Pallas kernels, per_device(): pl.pallas_call(kernel, out_shape=(jax.ShapeDtypeStruct((NB, NB, ROWS, BLO...  83.4 us
    pallas_call x1, Pallas kernels, per_device(): pl.pallas_call(hand_over, out_shape=[jax.ShapeDtypeStruct(x.shape, x.dtyp...  2.66 us

profile of v1, /device:TPU:9, one launch (start us, length us, event | category | flops | bytes accessed | tf_op | source)
XLA Modules:
  0.0 86.7 jit_solution(1128478813467507550)
XLA Ops:
  0.6 83.4 %shard_map.103 = (bf16[3,3,128,1024]{3,2,1,0:T(8,128)(2,1)}, f32[3,32,128]{2,1,0:T(8,128)}, bf16[128,3,2,128]{3,2,1,0:T(2,128)(2,1)}) custom-call(s32[9]{0:T(128)} %home.1, bf16[128,3,2,128]{3,2,1,0:T(2,128)(2,1)} %bitcast.9, bf16[3,3,128,1024]{3,2,1,0:T(8,128)(2,1)} %bitcast.7, bf16[3,128,1024]{2,1,0:T(8,128)(2,1)} %bitcast.8, ...), custom_call_target="tpu_custom_call" | custom-call | tf_op jit(solution)/shard_map/pallas_call | solution.py:567
  84.0 2.7 %shard_map.104 = (bf16[3,3,128,1024]{3,2,1,0:T(8,128)(2,1)}, f32[3,32,128]{2,1,0:T(8,128)}, bf16[128,3,2,128]{3,2,1,0:T(2,128)(2,1)}) custom-call(bf16[3,3,128,1024]{3,2,1,0:T(8,128)(2,1)} %get-tuple-element.9.upd, f32[3,32,128]{2,1,0:T(8,128)} %get-tuple-element.10.kgrad, bf16[128,3,2,128]{3,2,1,0:T(2,128)(2,1)} %get-tuple-element.11.ggrad), custom_call_target="tpu_custom_call" | custom-call | tf_op jit(solution)/shard_map/pallas_call | solution.py:643
